TPU v7x, 32 devices: a whole 2x2x4 slice. The times are simulated.
32 devices in a mesh: cuts: 2 (over core), tile: 16 (over z, y, x).
Axes of the slice: x: 2, y: 2, z: 4, core: 2. Of those that a mesh axis runs over, the one named last changes fastest.
Arguments:
- transmission: float32 [2, 2, 4096, 512], P(None, 'cuts', 'tile')
- illumination: float32 [2, 256, 256], replicated, may hold values from -6 to 6
- measured: float32 [16, 256, 256], P('tile'), may hold values from 0.2 to 5
- offsets: int32 [16, 2], P('tile'), may hold values from 0 to 256, as said below
- live_count: int32 [16], P('tile'), may hold values from 1 to 1, as said below
Outputs:
- object_grad: float32 [2, 2, 4096, 512], P(None, 'cuts', 'tile')
Inputs may be any that keep to these rules, and one draw needn't show every extreme that they name: offsets[j, 0] counts rows from the first row of tile j // 1 and may run past that tile's end (past the last tile, into the first); offsets[j, 1] counts columns; in every draw some live slot has row 255 and column 256. `live_count`: slots of a tile at or beyond its count are unused; some tile has all 1 slots used in every draw.
All inputs are finite; a program needn't handle non-finite values.
Results may differ from a plain program's by a relative error of at most 0.0049.
Values may be sent and summed in bfloat16 or wider, within the bound.
A program may use at most 64 MiB of HBM per device.

v0:
```python
import math

import jax
import jax.numpy as jnp
from jax import lax
from jax.sharding import PartitionSpec as P


def shifted(value, axis, steps):
    count = lax.axis_size(axis)
    pairs = [(source, (source + steps) % count) for source in range(count)]
    return lax.ppermute(value, axis, pairs)


def passed_along(value, axis, steps):
    count = lax.axis_size(axis)
    first, last = (max(0, -steps), min(count, count - steps))
    return lax.ppermute(value, axis, [(source, source + steps) for source in range(first, last)])


def fresnel_tables(patch_width):
    freq = jnp.arange(patch_width, dtype=jnp.int32)
    signed = jnp.where(freq < patch_width // 2, freq, freq - patch_width).astype(jnp.float32)
    phases = math.pi * signed * signed / (4.0 * patch_width)
    product = freq[:, None] * freq[None, :] % patch_width
    angles = 2.0 * math.pi * product.astype(jnp.float32) / patch_width
    cos_table = jnp.cos(angles)
    sin_table = jnp.sin(angles)
    shifted_real = jnp.cos(angles - phases[None, :])
    shifted_imag = jnp.sin(angles - phases[None, :])
    highest = lax.Precision.HIGHEST
    prop_real = (
        jnp.dot(shifted_real, cos_table, precision=highest)
        + jnp.dot(shifted_imag, sin_table, precision=highest)
    ) / patch_width
    prop_imag = (
        jnp.dot(shifted_imag, cos_table, precision=highest)
        - jnp.dot(shifted_real, sin_table, precision=highest)
    ) / patch_width
    factor = 1.0 / math.sqrt(patch_width)
    far_real = cos_table * factor
    far_imag = -sin_table * factor
    return (prop_real, prop_imag, far_real, far_imag)


def left_product(mat_real, mat_imag, real_part, imag_part):
    width = mat_real.shape[0]
    stacked = jnp.concatenate(
        [
            jnp.concatenate([mat_real, -mat_imag], axis=1),
            jnp.concatenate([mat_imag, mat_real], axis=1),
        ],
        axis=0,
    )
    values = jnp.concatenate([real_part, imag_part], axis=-2)
    result = jnp.einsum("ab,...bc->...ac", stacked, values, precision=lax.Precision.HIGHEST)
    return (result[..., :width, :], result[..., width:, :])


def right_product(real_part, imag_part, mat_real, mat_imag):
    width = mat_real.shape[1]
    stacked = jnp.concatenate(
        [
            jnp.concatenate([mat_real, mat_imag], axis=1),
            jnp.concatenate([-mat_imag, mat_real], axis=1),
        ],
        axis=0,
    )
    values = jnp.concatenate([real_part, imag_part], axis=-1)
    result = jnp.einsum("...ab,bc->...ac", values, stacked, precision=lax.Precision.HIGHEST)
    return (result[..., :width], result[..., width:])


def apply_forward(mat_real, mat_imag, real_part, imag_part):
    left_real, left_imag = left_product(mat_real, mat_imag, real_part, imag_part)
    return right_product(left_real, left_imag, mat_real.T, mat_imag.T)


def apply_adjoint(mat_real, mat_imag, real_part, imag_part):
    left_real, left_imag = left_product(mat_real.T, -mat_imag.T, real_part, imag_part)
    return right_product(left_real, left_imag, mat_real, -mat_imag)


def complex_times(first_real, first_imag, second_real, second_imag):
    return (
        first_real * second_real - first_imag * second_imag,
        first_real * second_imag + first_imag * second_real,
    )


def conj_times(first_real, first_imag, second_real, second_imag):
    return (
        first_real * second_real + first_imag * second_imag,
        first_real * second_imag - first_imag * second_real,
    )


def on_device(transmission, illumination, measured, offsets, live_count):
    cut_index = lax.axis_index("cuts")
    cut_count = lax.axis_size("cuts")
    slot_count = measured.shape[0]
    patch_width = illumination.shape[-1]
    slice_depth = transmission.shape[1]
    tile_rows = transmission.shape[2]
    prop_real, prop_imag, far_real, far_imag = fresnel_tables(patch_width)
    border = shifted(transmission, "tile", -1)
    extended = jnp.concatenate([transmission, border], axis=2)
    anchor = jnp.zeros((), jnp.int32)

    def cut_patch(row_offset, col_offset):
        return lax.dynamic_slice(
            extended,
            (anchor, anchor, row_offset, col_offset),
            (2, slice_depth, patch_width, patch_width),
        )

    patches = jax.vmap(cut_patch)(offsets[:, 0], offsets[:, 1])
    used_slots = live_count[0]
    live_flags = (jnp.arange(slot_count, dtype=jnp.int32) < used_slots).astype(jnp.float32)
    group_count = slot_count // slot_count
    cut_first = cut_index == 0
    cut_last = cut_index == cut_count - 1

    def forward_section(section_step, loop_state):
        arrived, kept_waves, exit_grad = loop_state
        micro_batch = section_step - cut_index
        active = (
            (micro_batch >= 0)
            & (micro_batch < group_count)
            & (micro_batch * slot_count < used_slots)
        )
        first_slot = jnp.clip(micro_batch, 0, group_count - 1) * slot_count

        def forward_compute_section(unused):
            incoming = arrived.astype(jnp.float32)
            wave_real = jnp.where(cut_first, illumination[0], incoming[:, 0])
            wave_imag = jnp.where(cut_first, illumination[1], incoming[:, 1])
            saved_list = [jnp.stack([wave_real, wave_imag], axis=1)]
            chi_real, chi_imag = complex_times(
                wave_real, wave_imag, patches[:, 0, 0], patches[:, 1, 0]
            )
            wave_real, wave_imag = apply_forward(prop_real, prop_imag, chi_real, chi_imag)
            kept_new = lax.dynamic_update_slice_in_dim(
                kept_waves, jnp.stack(saved_list, axis=1), first_slot, 0
            )

            def far_side(unused_far):
                out_real, out_imag = apply_forward(far_real, far_imag, wave_real, wave_imag)
                weight = (out_real * out_real + out_imag * out_imag - measured) * live_flags[
                    :, None, None
                ]
                back_real, back_imag = apply_adjoint(
                    far_real, far_imag, weight * out_real, weight * out_imag
                )
                return jnp.stack([back_real, back_imag], axis=1)

            def skip_far(unused_far):
                return jnp.zeros((slot_count, 2, patch_width, patch_width), jnp.float32)

            grad_group = lax.cond(cut_last, far_side, skip_far, None)
            outgoing = jnp.stack([wave_real, wave_imag], axis=1).astype(jnp.bfloat16)
            return (outgoing, kept_new, grad_group)

        def forward_pass_through(unused):
            return (jnp.zeros_like(arrived), kept_waves, exit_grad)

        outgoing, kept_waves, exit_grad = lax.cond(
            active, forward_compute_section, forward_pass_through, None
        )
        arrived = passed_along(outgoing, "cuts", 1)
        return (arrived, kept_waves, exit_grad)

    start_state = (
        jnp.zeros((slot_count, 2, patch_width, patch_width), jnp.bfloat16),
        jnp.zeros((slot_count, slice_depth, 2, patch_width, patch_width), jnp.float32),
        jnp.zeros((slot_count, 2, patch_width, patch_width), jnp.float32),
    )
    unused_wave, kept_waves, exit_grad = lax.fori_loop(
        0, cut_count + group_count - 1, forward_section, start_state
    )

    def backward_section(section_step, loop_state):
        arrived, patch_grads = loop_state
        micro_batch = section_step - (cut_count - 1 - cut_index)
        active = (
            (micro_batch >= 0)
            & (micro_batch < group_count)
            & (micro_batch * slot_count < used_slots)
        )
        first_slot = jnp.clip(micro_batch, 0, group_count - 1) * slot_count

        def backward_compute_section(unused):
            grad_wave = jnp.where(cut_last, exit_grad, arrived.astype(jnp.float32))
            grad_real = grad_wave[:, 0]
            grad_imag = grad_wave[:, 1]
            pieces = [None] * slice_depth
            for layer_index in reversed(range(slice_depth)):
                chi_real, chi_imag = apply_adjoint(prop_real, prop_imag, grad_real, grad_imag)
                pieces[layer_index] = jnp.stack(
                    conj_times(
                        kept_waves[:, layer_index, 0],
                        kept_waves[:, layer_index, 1],
                        chi_real,
                        chi_imag,
                    ),
                    axis=1,
                )
                grad_real, grad_imag = conj_times(
                    patches[:, 0, layer_index], patches[:, 1, layer_index], chi_real, chi_imag
                )
            grads_new = lax.dynamic_update_slice_in_dim(
                patch_grads, jnp.stack(pieces, axis=2), first_slot, 0
            )
            outgoing = jnp.stack([grad_real, grad_imag], axis=1).astype(jnp.bfloat16)
            return (outgoing, grads_new)

        def backward_pass_through(unused):
            return (jnp.zeros_like(arrived), patch_grads)

        outgoing, patch_grads = lax.cond(
            active, backward_compute_section, backward_pass_through, None
        )
        arrived = passed_along(outgoing, "cuts", -1)
        return (arrived, patch_grads)

    back_state = (
        jnp.zeros((slot_count, 2, patch_width, patch_width), jnp.bfloat16),
        jnp.zeros_like(patches),
    )
    unused_grad, patch_grads = lax.fori_loop(
        0, cut_count + group_count - 1, backward_section, back_state
    )

    def add_patch(slot_index, total):
        corner = (anchor, anchor, offsets[slot_index, 0], offsets[slot_index, 1])
        current = lax.dynamic_slice(total, corner, (2, slice_depth, patch_width, patch_width))
        return lax.dynamic_update_slice(total, current + patch_grads[slot_index], corner)

    summed = lax.fori_loop(0, slot_count, add_patch, jnp.zeros_like(extended))
    spill = shifted(summed[:, :, tile_rows:, :].astype(jnp.bfloat16), "tile", 1).astype(jnp.float32)
    own_rows = summed[:, :, :tile_rows, :]
    return jnp.concatenate([own_rows + spill, own_rows[:, :, patch_width:, :]], axis=2)


def solution(mesh):
    placed = (P(None, "cuts", "tile", None), P(), P("tile", None, None), P("tile", None), P("tile"))
    return jax.shard_map(
        on_device,
        mesh=mesh,
        in_specs=placed,
        out_specs=P(None, "cuts", "tile", None),
        check_vma=False,
    )
```

profile of v0, /device:TPU:0, one launch (start us, length us, event | category | flops | bytes accessed | tf_op | source)
XLA Modules:
  0.0 112.7 jit_solution(8805135938683972860)
XLA Ops:
  0.0 6.9 %collective-permute-start.2 = (f32[2,1,256,512]{3,2,1,0:T(8,128)}, f32[2,1,256,512]{3,2,1,0:T(8,128)S(1)}, u32[]{:S(2)}, u32[]{:S(2)}) collective-permute-start(f32[2,1,256,512]{3,2,1,0:T(8,128)} %param.15), channel_id=1, source_target_pairs={{0,15},{1,0},{2,1},{3,2},{4,3},{5,4},{6,5},{7,6},{8,7},{9,8},{10,9... | collective-permute-start | bytes 3145736 | tf_op jit(solution)/shard_map/ppermute | solution.py:12
  6.9 1.3 %fusion.130 = (s32[1,1]{1,0:T(1,128)}, s32[1,1]{1,0:T(1,128)}) fusion(s32[1,2]{1,0:T(1,128)} %param.18), kind=kLoop, calls=%fused_computation.184 | loop fusion | bytes 16 | tf_op jit(solution)/shard_map/slice | solution.py:117
  16.6 2.2 %fusion.90 = f32[256,256]{1,0:T(8,128)S(1)} fusion(f32[256]{0:T(256)S(1)} %fusion.105), kind=kOutput, calls=%fused_computation.152 | convolution fusion | flops 203227136 | bytes 263168 | tf_op jit(solution)/shard_map/dot_general | solution.py:33
  18.8 2.2 %fusion.89 = f32[256,256]{1,0:T(8,128)S(1)} fusion(f32[256]{0:T(256)S(1)} %fusion.105), kind=kOutput, calls=%fused_computation.151 | convolution fusion | flops 203227136 | bytes 263168 | tf_op jit(solution)/shard_map/dot_general | solution.py:37
  21.0 0.0 copy-start.3
  21.0 2.9 %fusion.79 = f32[256,256]{1,0:T(8,128)} fusion(f32[256,256]{1,0:T(8,128)S(1)} %fusion.90, f32[256]{0:T(256)S(1)} %fusion.105), kind=kOutput, calls=%fused_computation.133 | convolution fusion | flops 203358208 | bytes 525312 | tf_op jit(solution)/shard_map/dot_general | solution.py:34
  23.9 2.2 %fusion.80 = f32[256,256]{1,0:T(8,128)S(1)} fusion(f32[256,256]{1,0:T(8,128)S(1)} %fusion.89, f32[256]{0:T(256)S(1)} %fusion.105), kind=kOutput, calls=%fused_computation.135 | convolution fusion | flops 203358208 | bytes 525312 | tf_op jit(solution)/shard_map/dot_general | solution.py:38
  26.1 0.0 copy-start
  26.1 3.5 %collective-permute-done.2 = f32[2,1,256,512]{3,2,1,0:T(8,128)S(1)} collective-permute-done((f32[2,1,256,512]{3,2,1,0:T(8,128)}, f32[2,1,256,512]{3,2,1,0:T(8,128)S(1)}, u32[]{:S(2)}, u32[]{:S(2)}) %collective-permute-start.2) | collective-permute-done | bytes 1048608 | tf_op jit(solution)/shard_map/ppermute | solution.py:12
  29.7 0.0 copy-done.3
  29.7 0.4 fusion.82
  30.0 0.8 broadcast.58
  30.9 0.0 copy-done
  30.9 33.8 %while.46 = (s32[]{:T(128)}, bf16[1,2,256,256]{3,2,1,0:T(8,128)(2,1)S(1)}, f32[1,1,2,256,256]{4,3,2,1,0:T(8,128)S(1)}, f32[1,2,256,256]{3,2,1,0:T(8,128)}, s32[]...) while((s32[]{:T(128)}, ...), condition=%wide.region_5.6_spmd.clone.clone, body=%wide.region_0.5_spmd.clone.clone.sunk | while | flops 4840226816 | bytes 30933484 | solution.py:178
  31.1 0.1 fusion.132
  32.0 10.0 %conditional.9 = (bf16[1,2,256,256]{3,2,1,0:T(8,128)(2,1)S(1)}, f32[1,1,2,256,256]{4,3,2,1,0:T(8,128)S(1)}, f32[1,2,256,256]{3,2,1,0:T(8,128)}) conditional(s32[]{:T(128)} %convert_element_type.149, (f32[1,1,2,256,256]{4,3,2,1,0:T(8,128)S(1)}, f32[1,2,256,256]{3,2,1,0:T(8,128)}) %tuple.135, (pred[]{:T(512)}, f32[2,256,256]{2,1,0:T(8,128)}, ...), branch_computations={%region_1.1_spmd, %region_2.4_spmd.clone} | conditional | flops 4839309312 | bytes 29360250 | solution.py:167
  32.0 1.1 %fusion.69 = (f32[1,256,256]{2,1,0:T(8,128)S(1)}, f32[1,256,256]{2,1,0:T(8,128)S(1)}, f32[1,256,256]{2,1,0:T(8,128)S(1)}) fusion(f32[1,2,1,256,256]{4,3,2,1,0:T(8,128)S(1)} %get-tuple-element.800, f32[1,2,256,256]{3,2,1,0:T(8,128)S(1)} %convert_element_type.111, f32[2,256,256]{2,1,0:T(8,128)} %get-tuple-element.798, pred[]{:T(512)} %get-tuple-element.797), kind=kLoop, calls=%fused_computation.112 | loop fusion | flops 327680 | bytes 2359297 | tf_op jit(solution)/shard_map/while/body/eval_jaxpr/cond/branch_1_fun/sub | solution.py:86
  33.2 0.1 fusion.70
  33.3 2.9 %convolution_bitcast_fusion.7 = f32[1,512,256]{1,2,0:T(8,128)S(1)} fusion(f32[256,256]{1,0:T(8,128)} %get-tuple-element.801, f32[256,256]{1,0:T(8,128)S(1)} %get-tuple-element.802, f32[256,256]{1,0:T(8,128)S(1)} %neg.41, f32[1,256,256]{2,1,0:T(8,128)S(1)} %fusion.70, f32[1,256,256]{2,1,0:T(8,128)S(1)} %get-tuple-element.873), kind=kOutput, calls=%fused_computation.80 | convolution fusion | flops 806223872 | bytes 1835008 | tf_op jit(solution)/shard_map/while/body/eval_jaxpr/cond/branch_1_fun/ab,...bc->...ac/dot_general | solution.py:56
  36.2 2.9 %convolution_bitcast_fusion.6 = f32[1,256,512]{2,1,0:T(8,128)S(1)} fusion(f32[256,256]{0,1:T(8,128)} %bitcast.69, f32[256,256]{0,1:T(8,128)S(1)} %bitcast_negate_fusion.2, f32[256,256]{0,1:T(8,128)S(1)} %bitcast.177, f32[1,256,256]{1,2,0:T(8,128)S(1)} %get-tuple-element.899, f32[1,256,256]{1,2,0:T(8,128)S(1)} %get-tuple-element.898), kind=kOutput, calls=%fused_computation.79 | convolution fusion | flops 806223872 | bytes 1835008 | tf_op jit(solution)/shard_map/while/body/eval_jaxpr/cond/branch_1_fun/...ab,bc->...ac/dot_general | solution.py:70
  39.2 1.7 %fusion.68 = (f32[256,256]{1,0:T(8,128)S(1)}, f32[256,256]{1,0:T(8,128)S(1)}) fusion(f32[256,256]{1,0:T(8,128)S(1)} %get-tuple-element.807, f32[256,256]{1,0:T(8,128)S(1)} %get-tuple-element.808, f32[256,256]{1,0:T(8,128)S(1)} %get-tuple-element.807, f32[256,256]{1,0:T(8,128)S(1)} %get-tuple-element.808), kind=kLoop, calls=%fused_computation.108 | loop fusion | flops 196608 | bytes 1572864 | tf_op jit(solution)/shard_map/mul | solution.py:42
  41.0 0.8 conditional.5
  41.0 0.8 broadcast.47
  41.9 1.3 %collective-permute-start.1 = (bf16[1,2,256,256]{3,2,1,0:T(8,128)(2,1)S(1)}, bf16[1,2,256,256]{3,2,1,0:T(8,128)(2,1)S(1)}, u32[]{:S(2)}, u32[]{:S(2)}) collective-permute-start(bf16[1,2,256,256]{3,2,1,0:T(8,128)(2,1)S(1)} %get-tuple-element.1063), channel_id=1, source_target_pairs={{0,16},{1,17},{2,18},{3,19},{4,20},{5,21},{6,22},{7,23},{8,24},{9,... | collective-permute-start | bytes 786440 | tf_op jit(solution)/shard_map/while/body/eval_jaxpr/ppermute | solution.py:18
  43.2 1.1 collective-permute-done.1
  44.4 0.1 fusion.132
  45.2 0.1 conditional.9
  45.2 18.4 %collective-permute-start.1 = (bf16[1,2,256,256]{3,2,1,0:T(8,128)(2,1)S(1)}, bf16[1,2,256,256]{3,2,1,0:T(8,128)(2,1)S(1)}, u32[]{:S(2)}, u32[]{:S(2)}) collective-permute-start(bf16[1,2,256,256]{3,2,1,0:T(8,128)(2,1)S(1)} %get-tuple-element.1063), channel_id=1, source_target_pairs={{0,16},{1,17},{2,18},{3,19},{4,20},{5,21},{6,22},{7,23},{8,24},{9,... | collective-permute-start | bytes 786440 | tf_op jit(solution)/shard_map/while/body/eval_jaxpr/ppermute | solution.py:18
  63.6 1.1 collective-permute-done.1
  64.8 18.0 %while.45 = (s32[]{:T(128)}, bf16[1,2,256,256]{3,2,1,0:T(8,128)(2,1)S(1)}, f32[1,2,1,256,256]{4,3,1,2,0:T(8,128)S(1)}, s32[]{:T(128)}, s32[]{:T(128)}, /*index=5...) while((s32[]{:T(128)}, ...), condition=%wide.region_9.10_spmd, body=%wide.region_6.9_spmd.sunk | while | flops 1614020608 | bytes 13107488 | solution.py:230
  65.7 1.3 %collective-permute-start = (bf16[1,2,256,256]{3,2,1,0:T(8,128)(2,1)S(1)}, bf16[1,2,256,256]{3,2,1,0:T(8,128)(2,1)S(1)}, u32[]{:S(2)}, u32[]{:S(2)}) collective-permute-start(bf16[1,2,256,256]{3,2,1,0:T(8,128)(2,1)S(1)} %get-tuple-element.1047), channel_id=1, source_target_pairs={{16,0},{17,1},{18,2},{19,3},{20,4},{21,5},{22,6},{23,7},{24,8},{25... | collective-permute-start | bytes 786440 | tf_op jit(solution)/shard_map/while/body/eval_jaxpr/ppermute | solution.py:18
  67.0 7.0 %collective-permute-done = bf16[1,2,256,256]{3,2,1,0:T(8,128)(2,1)S(1)} collective-permute-done((bf16[1,2,256,256]{3,2,1,0:T(8,128)(2,1)S(1)}, bf16[1,2,256,256]{3,2,1,0:T(8,128)(2,1)S(1)}, u32[]{:S(2)}, u32[]{:S(2)}) %collective-permute-start) | collective-permute-done | bytes 262176 | tf_op jit(solution)/shard_map/while/body/eval_jaxpr/ppermute | solution.py:18
  74.7 4.6 %conditional.8 = (bf16[1,2,256,256]{3,2,1,0:T(8,128)(2,1)S(1)}, f32[1,2,1,256,256]{4,3,1,2,0:T(8,128)S(1)}) conditional(s32[]{:T(128)} %convert_element_type.147, f32[1,2,1,256,256]{4,3,1,2,0:T(8,128)S(1)} %get-tuple-element.1142, (f32[1,2,1,256,256]{4,3,2,1,0:T(8,128)S(1)}, pred[]{:T(512)}, bf16[1,2,256,256]{3,2,1,0:T(8,128)(2,1)S(1)}, ...), branch_computations={%region_7.7_spmd, %region_8.8_spmd} | conditional | flops 1614020608 | bytes 12058641 | solution.py:220
  74.7 0.1 convert_select_fusion
  74.9 2.1 %convolution_bitcast_fusion.5 = f32[1,512,256]{1,2,0:T(8,128)S(1)} fusion(f32[256,256]{0,1:T(8,128)} %bitcast.38, f32[256,256]{0,1:T(8,128)S(1)} %bitcast_negate_fusion.1, f32[256,256]{0,1:T(8,128)S(1)} %bitcast.178, f32[1,256,256]{2,1,0:T(8,128)S(1)} %get-tuple-element.893, f32[1,256,256]{2,1,0:T(8,128)S(1)} %get-tuple-element.892), kind=kOutput, calls=%fused_computation.32 | convolution fusion | flops 806223872 | bytes 1835008 | tf_op jit(solution)/shard_map/while/body/eval_jaxpr/cond/branch_1_fun/ab,...bc->...ac/dot_general | solution.py:56
  77.0 2.1 %convolution_bitcast_fusion.4 = f32[1,256,512]{2,1,0:T(8,128)S(1)} fusion(f32[256,256]{1,0:T(8,128)} %get-tuple-element.678, f32[256,256]{1,0:T(8,128)S(1)} %get-tuple-element.679, f32[256,256]{1,0:T(8,128)S(1)} %neg.31, f32[1,256,256]{1,2,0:T(8,128)S(1)} %get-tuple-element.891, f32[1,256,256]{1,2,0:T(8,128)S(1)} %get-tuple-element.890), kind=kOutput, calls=%fused_computation.31 | convolution fusion | flops 806223872 | bytes 1835008 | tf_op jit(solution)/shard_map/while/body/eval_jaxpr/cond/branch_1_fun/...ab,bc->...ac/dot_general | solution.py:70
  79.1 0.1 fusion.37
  79.3 1.3 %collective-permute-start = (bf16[1,2,256,256]{3,2,1,0:T(8,128)(2,1)S(1)}, bf16[1,2,256,256]{3,2,1,0:T(8,128)(2,1)S(1)}, u32[]{:S(2)}, u32[]{:S(2)}) collective-permute-start(bf16[1,2,256,256]{3,2,1,0:T(8,128)(2,1)S(1)} %get-tuple-element.1047), channel_id=1, source_target_pairs={{16,0},{17,1},{18,2},{19,3},{20,4},{21,5},{22,6},{23,7},{24,8},{25... | collective-permute-start | bytes 786440 | tf_op jit(solution)/shard_map/while/body/eval_jaxpr/ppermute | solution.py:18
  80.6 2.1 %collective-permute-done = bf16[1,2,256,256]{3,2,1,0:T(8,128)(2,1)S(1)} collective-permute-done((bf16[1,2,256,256]{3,2,1,0:T(8,128)(2,1)S(1)}, bf16[1,2,256,256]{3,2,1,0:T(8,128)(2,1)S(1)}, u32[]{:S(2)}, u32[]{:S(2)}) %collective-permute-start) | collective-permute-done | bytes 262176 | tf_op jit(solution)/shard_map/while/body/eval_jaxpr/ppermute | solution.py:18
  82.8 0.0 copy-start.1
  82.8 0.8 copy-done.1
  83.6 0.0 copy-start.2
  83.6 0.2 broadcast_in_dim.23
  83.8 0.8 copy-done.2
  84.6 8.2 %dynamic_update_slice.6 = f32[2,1,512,512]{3,2,1,0:T(8,128)S(1)} dynamic-update-slice(f32[2,1,512,512]{3,2,1,0:T(8,128)S(1)} %broadcast_in_dim.23, f32[2,1,256,256]{3,2,1,0:T(8,128)S(1)} %bitcast.185, s32[]{:T(128)} %constant.97.clone.1, s32[]{:T(128)} %constant.97.clone.1, s32[]{:T(128)S(6)} %select_n.98, s32[]{:T(128)S(6)} %select_n.99) | dynamic-update-slice | bytes 1048580 | tf_op jit(solution)/shard_map/while/body/eval_jaxpr/dynamic_update_slice | solution.py:237
  92.8 0.1 slice.232
  92.9 0.1 collective-permute-start.3
  93.0 18.6 %collective-permute-done.3 = bf16[2,1,256,512]{3,2,1,0:T(8,128)(2,1)S(1)} collective-permute-done((bf16[2,1,256,512]{3,2,1,0:T(8,128)(2,1)S(1)}, bf16[2,1,256,512]{3,2,1,0:T(8,128)(2,1)S(1)}, u32[]{:S(2)}, u32[]{:S(2)}) %collective-permute-start.3) | collective-permute-done | bytes 524320 | tf_op jit(solution)/shard_map/ppermute | solution.py:12
  111.6 1.1 %slice_add_fusion = f32[2,1,256,512]{3,2,1,0:T(8,128)} fusion(f32[2,1,512,512]{3,2,1,0:T(8,128)S(1)} %dynamic_update_slice.6, bf16[2,1,256,512]{3,2,1,0:T(8,128)(2,1)S(1)} %collective-permute-done.3), kind=kLoop, calls=%fused_computation.137 | loop fusion | flops 524288 | bytes 2621440 | tf_op jit(solution)/shard_map/add | solution.py:242
  (24 shorter events, 0.7 us)
Async XLA Ops:
  0.0 29.7 %collective-permute-start.2 = (f32[2,1,256,512]{3,2,1,0:T(8,128)}, f32[2,1,256,512]{3,2,1,0:T(8,128)S(1)}, u32[]{:S(2)}, u32[]{:S(2)}) collective-permute-start(f32[2,1,256,512]{3,2,1,0:T(8,128)} %param.15), channel_id=1, source_target_pairs={{0,15},{1,0},{2,1},{3,2},{4,3},{5,4},{6,5},{7,6},{8,7},{9,8},{10,9... | collective-permute-start | bytes 3145736 | tf_op jit(solution)/shard_map/ppermute | solution.py:12
  21.0 8.7 %copy-start.3 = (f32[2,1,256,512]{3,2,1,0:T(8,128)S(1)}, f32[2,1,256,512]{3,2,1,0:T(8,128)}, u32[]{:S(2)}) copy-start(f32[2,1,256,512]{3,2,1,0:T(8,128)} %param.15) | copy-start | bytes 3145732
  26.1 4.8 %copy-start = (f32[1,256,256]{2,1,0:T(8,128)S(1)}, f32[1,256,256]{2,1,0:T(8,128)}, u32[]{:S(2)}) copy-start(f32[1,256,256]{2,1,0:T(8,128)} %param.17) | copy-start | bytes 786436
  41.9 2.4 %collective-permute-start.1 = (bf16[1,2,256,256]{3,2,1,0:T(8,128)(2,1)S(1)}, bf16[1,2,256,256]{3,2,1,0:T(8,128)(2,1)S(1)}, u32[]{:S(2)}, u32[]{:S(2)}) collective-permute-start(bf16[1,2,256,256]{3,2,1,0:T(8,128)(2,1)S(1)} %get-tuple-element.1063), channel_id=1, source_target_pairs={{0,16},{1,17},{2,18},{3,19},{4,20},{5,21},{6,22},{7,23},{8,24},{9,... | collective-permute-start | bytes 786440 | tf_op jit(solution)/shard_map/while/body/eval_jaxpr/ppermute | solution.py:18
  45.2 19.5 %collective-permute-start.1 = (bf16[1,2,256,256]{3,2,1,0:T(8,128)(2,1)S(1)}, bf16[1,2,256,256]{3,2,1,0:T(8,128)(2,1)S(1)}, u32[]{:S(2)}, u32[]{:S(2)}) collective-permute-start(bf16[1,2,256,256]{3,2,1,0:T(8,128)(2,1)S(1)} %get-tuple-element.1063), channel_id=1, source_target_pairs={{0,16},{1,17},{2,18},{3,19},{4,20},{5,21},{6,22},{7,23},{8,24},{9,... | collective-permute-start | bytes 786440 | tf_op jit(solution)/shard_map/while/body/eval_jaxpr/ppermute | solution.py:18
  65.7 8.3 %collective-permute-start = (bf16[1,2,256,256]{3,2,1,0:T(8,128)(2,1)S(1)}, bf16[1,2,256,256]{3,2,1,0:T(8,128)(2,1)S(1)}, u32[]{:S(2)}, u32[]{:S(2)}) collective-permute-start(bf16[1,2,256,256]{3,2,1,0:T(8,128)(2,1)S(1)} %get-tuple-element.1047), channel_id=1, source_target_pairs={{16,0},{17,1},{18,2},{19,3},{20,4},{21,5},{22,6},{23,7},{24,8},{25... | collective-permute-start | bytes 786440 | tf_op jit(solution)/shard_map/while/body/eval_jaxpr/ppermute | solution.py:18
  79.3 3.4 %collective-permute-start = (bf16[1,2,256,256]{3,2,1,0:T(8,128)(2,1)S(1)}, bf16[1,2,256,256]{3,2,1,0:T(8,128)(2,1)S(1)}, u32[]{:S(2)}, u32[]{:S(2)}) collective-permute-start(bf16[1,2,256,256]{3,2,1,0:T(8,128)(2,1)S(1)} %get-tuple-element.1047), channel_id=1, source_target_pairs={{16,0},{17,1},{18,2},{19,3},{20,4},{21,5},{22,6},{23,7},{24,8},{25... | collective-permute-start | bytes 786440 | tf_op jit(solution)/shard_map/while/body/eval_jaxpr/ppermute | solution.py:18
  82.8 0.8 copy-start.1
  83.6 1.0 copy-start.2
  92.9 18.7 %collective-permute-start.3 = (bf16[2,1,256,512]{3,2,1,0:T(8,128)(2,1)S(1)}, bf16[2,1,256,512]{3,2,1,0:T(8,128)(2,1)S(1)}, u32[]{:S(2)}, u32[]{:S(2)}) collective-permute-start(bf16[2,1,256,512]{3,2,1,0:T(8,128)(2,1)S(1)} %slice.232), channel_id=1, source_target_pairs={{0,1},{1,2},{2,3},{3,4},{4,5},{5,6},{6,7},{7,8},{8,9},{9,10},{10,1... | collective-permute-start | bytes 1572872 | tf_op jit(solution)/shard_map/ppermute | solution.py:12
where the time goes:
time: 113 us
  waiting for transfers between devices  33.5 us (30%)
  starting transfers between devices  29.3 us (26%)
  matrix products  19.4 us (17%)
  local copies, waits for them, and re-layouts  13.4 us (12%)
  between operations  8.45 us (7%)
  other arithmetic  5.16 us (5%)
  loops' own time  3.45 us (3%)
    ppermute x4, starting transfers between devices, passed_along(): lax.ppermute(value, axis, [(source, source + steps) for source in range(f...  22.2 us
    ppermute x2, waiting for transfers between devices, shifted(): return lax.ppermute(value, axis, pairs)  22.1 us
    ppermute x4, waiting for transfers between devices, passed_along(): lax.ppermute(value, axis, [(source, source + steps) for source in range(f...  11.4 us
    dynamic_update_slice x1, local copies, waits for them, and re-layouts, add_patch(): lax.dynamic_update_slice(total, current + patch_grads[slot_index], corner)  8.2 us
    ppermute x2, starting transfers between devices, shifted(): return lax.ppermute(value, axis, pairs)  7.03 us
    dot_general x2, matrix products, right_product(): jnp.einsum('...ab,bc->...ac', values, stacked, precision=lax.Precision.HI...  4.98 us
    dot_general x2, matrix products, left_product(): jnp.einsum('ab,...bc->...ac', stacked, values, precision=lax.Precision.HI...  4.98 us
    dot_general x1, matrix products, fresnel_tables(): jnp.dot(shifted_imag, sin_table, precision=highest)  2.9 us
  transfers between devices with their start and end apart: 6, of which 6 were waited for; matrix products, arithmetic and copies ran while one was open for 10% of the time, Pallas kernels for 0%

commit v1 on v0

v1 whole, which is shorter than its diff:
```python
import functools
import math

import jax
import jax.numpy as jnp
import ml_dtypes
import numpy as np
from jax import lax
from jax.experimental import pallas as pl
from jax.experimental.pallas import tpu as pltpu
from jax.sharding import PartitionSpec as P

MESH = pl.DeviceIdType.MESH
F32 = jnp.float32
BF16 = jnp.bfloat16


def split_pair(value):
    high = value.astype(ml_dtypes.bfloat16)
    low = (value - high.astype(np.float64)).astype(ml_dtypes.bfloat16)
    return high, low


def constant_tables(width):
    freq = np.arange(width)
    signed = np.where(freq < width // 2, freq, freq - width).astype(np.float64)
    phases = math.pi * signed * signed / (4.0 * width)
    waves = np.exp(2j * math.pi * (freq[:, None] * freq[None, :] % width) / width)
    prop = (waves * np.exp(-1j * phases)[None, :]) @ waves.conj().T / width
    far = waves.conj() / math.sqrt(width)
    rows = []
    for mat in (prop, far):
        right = np.block([[mat.real, mat.imag], [-mat.imag, mat.real]])
        left = np.block([[mat.real, -mat.imag], [mat.imag, mat.real]])
        rows.append(np.stack(split_pair(right) + split_pair(left)))
    return np.stack(rows)


def halves(value):
    high = value.astype(BF16)
    low = (value - high.astype(F32)).astype(BF16)
    return high, low


def dot(a, b):
    return jnp.dot(a, b, preferred_element_type=F32)


def from_right(value, mats, at):
    high, low = halves(value)
    return dot(high, mats[at]) + (dot(low, mats[at]) + dot(high, mats[at + 1]))


def from_left(value, mats, at):
    high, low = halves(value)
    return dot(mats[at], high) + (dot(mats[at], low) + dot(mats[at + 1], high))


def beside(stacked):
    width = stacked.shape[0] // 2
    return jnp.concatenate([stacked[:width], stacked[width:]], axis=1)


def above(flat):
    width = flat.shape[1] // 2
    return jnp.concatenate([flat[:, :width], flat[:, width:]], axis=0)


def times(ar, ai, br, bi):
    return ar * br - ai * bi, ar * bi + ai * br


def conj_times(ar, ai, br, bi):
    return ar * br + ai * bi, ar * bi - ai * br


def one_hot(shape, along, offset, start=0):
    ahead = lax.broadcasted_iota(jnp.int32, shape, along) + start
    gap = ahead - lax.broadcasted_iota(jnp.int32, shape, 1 - along)
    return jnp.where(gap == offset, 1.0, 0.0).astype(BF16)


def moved_right(value, mask):
    high, low = halves(value)
    return dot(high, mask) + dot(low, mask)


def moved_left(mask, value):
    high, low = halves(value)
    return dot(mask, high) + dot(mask, low)


def kernel(
    tiles,
    trans_hbm,
    illum_hbm,
    measured_hbm,
    offs_hbm,
    live_hbm,
    tables,
    out,
    trans,
    illum,
    measured,
    offs,
    live,
    mats,
    off_out,
    off_in,
    code_out,
    code_in,
    level_out,
    level_in,
    wave,
    back,
    wave_out,
    back_out,
    grads,
    spill_out,
    spill_in,
    local_sem,
    send_sem,
    recv_sem,
):
    cut = lax.axis_index("cuts")
    tile = lax.axis_index("tile")
    before = lax.rem(tile + tiles - 1, tiles)
    after = lax.rem(tile + 1, tiles)
    other = 1 - cut
    rows, cols = trans.shape[1], trans.shape[2]
    width = illum.shape[1]

    barrier = pltpu.get_barrier_semaphore()
    for target in ((cut, before), (cut, after), (other, tile)):
        pl.semaphore_signal(barrier, inc=1, device_id=target, device_id_type=MESH)
    local = []
    for source, target in (
        (offs_hbm, offs),
        (live_hbm, live),
        (trans_hbm, trans),
        (illum_hbm, illum),
        (measured_hbm, measured),
        (tables.at[cut], mats),
    ):
        copy = pltpu.make_async_copy(source, target, local_sem.at[len(local)])
        copy.start()
        local.append(copy)
    local[0].wait()
    row_at = offs[0:1, 0:1]
    col_at = offs[0:1, 1:2]
    off_out[...] = jnp.broadcast_to(col_at, off_out.shape)
    pl.semaphore_wait(barrier, 3)

    def remote(src, dst, at, target):
        return pltpu.make_async_remote_copy(
            src_ref=src,
            dst_ref=dst,
            send_sem=send_sem.at[at],
            recv_sem=recv_sem.at[at],
            device_id=target,
            device_id_type=MESH,
        )

    off_copy = remote(off_out, off_in, 0, (cut, after))
    off_copy.start()
    for copy in local[1:]:
        copy.wait()
    flag = jnp.where(live[0:1, 0:1] > 0, 1.0, 0.0)
    own = jnp.concatenate([trans[0], trans[1]], axis=0)
    high, low = halves(own)
    off_copy.wait()
    next_at = off_in[0:1, 0:1]
    pick = one_hot((cols, width), 0, next_at)
    picked = dot(high, pick) + dot(low, pick)
    level = jnp.maximum(jnp.max(jnp.abs(picked), axis=0, keepdims=True), 1e-30) * (1.0 / 32767.0)
    level_out[...] = jnp.broadcast_to(level, level_out.shape)
    level_copy = remote(level_out, level_in, 1, (cut, before))
    level_copy.start()
    code_out[...] = jnp.round(picked / level).astype(jnp.int32).astype(jnp.int16)
    code_copy = remote(code_out, code_in, 2, (cut, before))
    code_copy.start()

    pick = one_hot((cols, width), 0, col_at)
    mine = beside(dot(high, pick) + dot(low, pick))
    mine = moved_left(one_hot((width, rows), 1, row_at), mine)
    row_pick = one_hot((width, rows), 1, row_at, rows)
    level_copy.wait()
    code_copy.wait()
    theirs = code_in[...].astype(jnp.int32).astype(F32) * level_in[0:1]
    patch = mine + moved_left(row_pick, beside(theirs))
    obj_r, obj_i = patch[:, :width], patch[:, width:]

    wave_copy = remote(wave_out, wave, 3, (1, tile))
    back_copy = remote(back_out, back, 4, (0, tile))

    def keep_grads(psi_r, psi_i, h_r, h_i):
        grad_r, grad_i = conj_times(psi_r, psi_i, h_r, h_i)
        grads[:, :width] = grad_r
        grads[:, width:] = grad_i

    @pl.when(cut == 0)
    def first():
        chi_r, chi_i = times(illum[0], illum[1], obj_r, obj_i)
        value = from_left(jnp.concatenate([chi_r, chi_i], axis=0), mats, 2)
        value = from_right(beside(value), mats, 0)
        wave_out[...] = value.astype(BF16)
        wave_copy.start()
        wave_copy.wait_send()
        back_copy.wait_recv()
        grad = back[...]
        value = dot(grad, mats[2]) + dot(grad, mats[3])
        value = from_left(above(value), mats, 0)
        keep_grads(illum[0], illum[1], value[:width], value[width:])

    @pl.when(cut == 1)
    def second():
        wave_copy.wait_recv()
        psi = wave[...].astype(F32)
        psi_r, psi_i = psi[:, :width], psi[:, width:]
        chi_r, chi_i = times(psi_r, psi_i, obj_r, obj_i)
        value = from_right(jnp.concatenate([chi_r, chi_i], axis=1), mats, 0)
        value = from_left(above(value), mats, 2)
        out_r, out_i = value[:width], value[width:]
        weight = (out_r * out_r + out_i * out_i - measured[0]) * flag
        value = jnp.concatenate([weight * out_r, weight * out_i], axis=0)
        value = from_left(value, mats, 0)
        value = from_right(beside(value), mats, 2)
        h_r, h_i = value[:, :width], value[:, width:]
        g_r, g_i = conj_times(obj_r, obj_i, h_r, h_i)
        back_out[...] = jnp.concatenate([g_r, g_i], axis=1).astype(BF16)
        back_copy.start()
        keep_grads(psi_r, psi_i, h_r, h_i)
        back_copy.wait_send()

    total = grads[...]
    high, low = halves(total)
    spill_out[...] = dot(one_hot((rows, width), 0, row_at, rows), high).astype(BF16)
    spill = remote(spill_out, spill_in, 5, (cut, after))
    spill.start()
    row_put = one_hot((rows, width), 0, row_at)
    kept = above(dot(row_put, high) + dot(row_put, low))
    kept = moved_right(kept, one_hot((width, cols), 1, col_at))
    put = one_hot((width, cols), 1, off_in[0:1, 0:1])
    spill.wait()
    for part in range(2):
        arrived = dot(spill_in[:, part * width : (part + 1) * width], put)
        out[part] = kept[part * rows : (part + 1) * rows] + arrived


def on_device(tiles, tables, transmission, illumination, measured, offsets, live_count):
    width = illumination.shape[-1]
    trans = transmission[:, 0]
    rows, cols = trans.shape[1:]
    hbm = pl.BlockSpec(memory_space=pltpu.HBM)
    total = pl.pallas_call(
        functools.partial(kernel, tiles),
        out_shape=jax.ShapeDtypeStruct(trans.shape, F32),
        in_specs=[hbm] * 6,
        out_specs=pl.BlockSpec(memory_space=pltpu.VMEM),
        scratch_shapes=[
            pltpu.VMEM(trans.shape, F32),
            pltpu.VMEM(illumination.shape, F32),
            pltpu.VMEM(measured.shape, F32),
            pltpu.VMEM((1, 2), jnp.int32),
            pltpu.VMEM((1, 1), jnp.int32),
            pltpu.VMEM((4, 2 * width, 2 * width), BF16),
            pltpu.VMEM((8, 128), jnp.int32),
            pltpu.VMEM((8, 128), jnp.int32),
            pltpu.VMEM((2 * rows, width), jnp.int16),
            pltpu.VMEM((2 * rows, width), jnp.int16),
            pltpu.VMEM((8, width), F32),
            pltpu.VMEM((8, width), F32),
            pltpu.VMEM((width, 2 * width), BF16),
            pltpu.VMEM((width, 2 * width), BF16),
            pltpu.VMEM((width, 2 * width), BF16),
            pltpu.VMEM((width, 2 * width), BF16),
            pltpu.VMEM((width, 2 * width), F32),
            pltpu.VMEM((rows, 2 * width), BF16),
            pltpu.VMEM((rows, 2 * width), BF16),
            pltpu.SemaphoreType.DMA((6,)),
            pltpu.SemaphoreType.DMA((6,)),
            pltpu.SemaphoreType.DMA((6,)),
        ],
        compiler_params=pltpu.CompilerParams(
            collective_id=0, has_side_effects=True, vmem_limit_bytes=48 * 1024 * 1024
        ),
    )(trans, illumination, measured, offsets, live_count[:, None], jnp.asarray(tables))
    return total[:, None]


def solution(mesh):
    placed = (P(None, "cuts", "tile", None), P(), P("tile", None, None), P("tile", None), P("tile"))
    tiles = mesh.shape["tile"]

    def whole(transmission, illumination, measured, offsets, live_count):
        tables = constant_tables(illumination.shape[-1])
        return jax.shard_map(
            functools.partial(on_device, tiles, tables),
            mesh=mesh,
            in_specs=placed,
            out_specs=P(None, "cuts", "tile", None),
            check_vma=False,
        )(transmission, illumination, measured, offsets, live_count)

    return whole
```

time: 113 us -> 41.9 us (0.37)
  Pallas kernels: 0 us -> 36.1 us
  waiting for transfers between devices: 33.5 us -> 0 us
  starting transfers between devices: 29.3 us -> 0 us
  matrix products: 19.4 us -> 0 us
  local copies, waits for them, and re-layouts: 13.4 us -> 4.84 us
  between operations: 8.45 us -> 0.67 us
  other arithmetic: 5.16 us -> 0 us
  loops' own time: 3.45 us -> 0 us
    pallas_call x0 -> x1, Pallas kernels: none -> 36.1 us  [on_device(): pl.pallas_call(functools.partial(kernel, tiles), out_shape=jax.ShapeDtype...]
    ppermute x6 -> x0, waiting for transfers between devices: 33.5 us -> none  [the longest x2 22.1 us: shifted(): return lax.ppermute(value, axis, pairs)]
    ppermute x6 -> x0, starting transfers between devices: 29.3 us -> none  [the longest x4 22.2 us: passed_along(): lax.ppermute(value, axis, [(source, source + steps) for source in range(f...]
    dot_general x8 -> x0, matrix products: 19.4 us -> none  [the longest x2 4.98 us: right_product(): jnp.einsum('...ab,bc->...ac', values, stacked, precision=lax.Precision.HI...]
    dynamic_update_slice x1 -> x0, local copies, waits for them, and re-layouts: 8.2 us -> none  [add_patch(): lax.dynamic_update_slice(total, current + patch_grads[slot_index], corner)]
    another operation x7 -> x0, loops' own time: 3.45 us -> none  [the longest x1 1.59 us: on_device(): lax.fori_loop(0, cut_count + group_count - 1, backward_section, back_state)]
    unnamed x8 -> x9, local copies, waits for them, and re-layouts: 1.59 us -> 4.84 us
    another operation x9 -> x0, local copies, waits for them, and re-layouts: 1.81 us -> none
  transfers between devices with their start and end apart: 6 -> 0, of which waited for: 6 -> 0; matrix products, arithmetic and copies ran while one was open for 10% -> 0% of each run, Pallas kernels for 0% -> 0%
where the time goes in v1:
time: 41.9 us; the launch traced here: 41.6 us
  Pallas kernels  36.1 us (86%)
  local copies, waits for them, and re-layouts  4.84 us (12%)
  between operations  0.67 us (2%)
    pallas_call x1, Pallas kernels, on_device(): pl.pallas_call(functools.partial(kernel, tiles), out_shape=jax.ShapeDtype...  36.1 us
    unnamed x9, local copies, waits for them, and re-layouts  4.84 us

profile of v1, /device:TPU:0, one launch (start us, length us, event | category | flops | bytes accessed | tf_op | source)
XLA Modules:
  0.0 41.6 jit_solution(6855880583072374670)
XLA Ops:
  0.7 0.0 copy-start
  0.7 1.2 %copy-done = f32[2,1,256,512]{3,2,1,0:T(8,128)S(1)} copy-done((f32[2,1,256,512]{3,2,1,0:T(8,128)S(1)}, f32[2,1,256,512]{3,2,1,0:T(8,128)}, u32[]{:S(2)}) %copy-start) | copy-done | bytes 1048600
  1.9 0.0 copy-start.1
  1.9 1.0 %copy-done.1 = f32[2,256,256]{2,1,0:T(8,128)S(1)} copy-done((f32[2,256,256]{2,1,0:T(8,128)S(1)}, f32[2,256,256]{2,1,0:T(8,128)}, u32[]{:S(2)}) %copy-start.1) | copy-done | bytes 524312
  2.9 0.0 copy-start.2
  2.9 0.9 %copy-done.2 = f32[1,256,256]{2,1,0:T(8,128)S(1)} copy-done((f32[1,256,256]{2,1,0:T(8,128)S(1)}, f32[1,256,256]{2,1,0:T(8,128)}, u32[]{:S(2)}) %copy-start.2) | copy-done | bytes 262168
  3.9 0.0 copy-start.3
  3.9 0.7 %copy-done.3 = s32[1,2]{1,0:T(1,128)S(1)} copy-done((s32[1,2]{1,0:T(1,128)S(1)}, s32[1,2]{1,0:T(1,128)}, u32[]{:S(2)}) %copy-start.3) | copy-done | bytes 32
  4.5 36.1 %shard_map.64 = f32[2,256,512]{2,1,0:T(8,128)S(1)} custom-call(f32[2,256,512]{2,1,0:T(8,128)S(1)} %bitcast.7, f32[2,256,256]{2,1,0:T(8,128)S(1)} %copy-done.1, f32[1,256,256]{2,1,0:T(8,128)S(1)} %copy-done.2, s32[1,2]{1,0:T(1,128)S(1)} %copy-done.3, s32[1,1]{1,0:T(1,128)} %bitcast.5.live_hbm, bf16[2,4,512,512]{3,2,1,0:T(8,128)(2,1)} %constant.2.clone.tables), custom_call_target="tpu_custom_call" | custom-call | tf_op jit(solution)/shard_map/pallas_call | solution.py:255
  40.7 1.0 %copy.10 = f32[2,1,256,512]{3,2,1,0:T(8,128)} copy(f32[2,1,256,512]{3,2,1,0:T(8,128)S(1)} %bitcast.6) | data formatting | bytes 2097152
Async XLA Ops:
  0.7 1.2 %copy-start = (f32[2,1,256,512]{3,2,1,0:T(8,128)S(1)}, f32[2,1,256,512]{3,2,1,0:T(8,128)}, u32[]{:S(2)}) copy-start(f32[2,1,256,512]{3,2,1,0:T(8,128)} %param.6) | copy-start | bytes 3145732
  1.9 1.0 %copy-start.1 = (f32[2,256,256]{2,1,0:T(8,128)S(1)}, f32[2,256,256]{2,1,0:T(8,128)}, u32[]{:S(2)}) copy-start(f32[2,256,256]{2,1,0:T(8,128)} %illum_hbm.1) | copy-start | bytes 1572868
  2.9 0.9 %copy-start.2 = (f32[1,256,256]{2,1,0:T(8,128)S(1)}, f32[1,256,256]{2,1,0:T(8,128)}, u32[]{:S(2)}) copy-start(f32[1,256,256]{2,1,0:T(8,128)} %measured_hbm.1) | copy-start | bytes 786436
  3.9 0.7 %copy-start.3 = (s32[1,2]{1,0:T(1,128)S(1)}, s32[1,2]{1,0:T(1,128)}, u32[]{:S(2)}) copy-start(s32[1,2]{1,0:T(1,128)} %offs_hbm.1) | copy-start | bytes 28

commit v2 on v1

--- a/solution.py
+++ b/solution.py
@@ -13,6 +13,8 @@
 MESH = pl.DeviceIdType.MESH
 F32 = jnp.float32
 BF16 = jnp.bfloat16
+MIDDLE = 2.6
+SCALE = 13650.0
 
 
 def split_pair(value):
@@ -118,6 +120,9 @@
     grads,
     spill_out,
     spill_in,
+    target_out,
+    target_in,
+    turn_sem,
     local_sem,
     send_sem,
     recv_sem,
@@ -131,7 +136,7 @@
     width = illum.shape[1]
 
     barrier = pltpu.get_barrier_semaphore()
-    for target in ((cut, before), (cut, after), (other, tile)):
+    for target in ((cut, before), (other, tile)):
         pl.semaphore_signal(barrier, inc=1, device_id=target, device_id_type=MESH)
     local = []
     for source, target in (
@@ -146,10 +151,18 @@
         copy.start()
         local.append(copy)
     local[0].wait()
+    local[1].wait()
     row_at = offs[0:1, 0:1]
     col_at = offs[0:1, 1:2]
-    off_out[...] = jnp.broadcast_to(col_at, off_out.shape)
-    pl.semaphore_wait(barrier, 3)
+    line = lax.broadcasted_iota(jnp.int32, off_out.shape, 0)
+    off_out[...] = jnp.where(line == 0, row_at, jnp.where(line == 1, col_at, live[0:1, 0:1]))
+    local[2].wait()
+    pick = one_hot((cols, width), 0, col_at)
+    picked = moved_right(jnp.concatenate([trans[0], trans[1]], axis=0), pick)
+    level = jnp.maximum(jnp.max(jnp.abs(picked), axis=0, keepdims=True), 1e-30) * (1.0 / 32767.0)
+    level_out[...] = jnp.broadcast_to(level, level_out.shape)
+    code_out[...] = jnp.round(picked / level).astype(jnp.int32).astype(jnp.int16)
+    pl.semaphore_wait(barrier, 2)
 
     def remote(src, dst, at, target):
         return pltpu.make_async_remote_copy(
@@ -163,29 +176,42 @@
 
     off_copy = remote(off_out, off_in, 0, (cut, after))
     off_copy.start()
-    for copy in local[1:]:
-        copy.wait()
-    flag = jnp.where(live[0:1, 0:1] > 0, 1.0, 0.0)
-    own = jnp.concatenate([trans[0], trans[1]], axis=0)
-    high, low = halves(own)
+    level_copy = remote(level_out, level_in, 1, (cut, after))
+    level_copy.start()
+    code_copy = remote(code_out, code_in, 2, (cut, after))
+    target_copy = remote(target_out, target_in, 6, (1, after))
+
+    @pl.when(cut == 0)
+    def send_first():
+        code_copy.start()
+        code_copy.wait_send()
+        pl.semaphore_signal(turn_sem, inc=1, device_id=(other, tile), device_id_type=MESH)
+
+    @pl.when(cut == 1)
+    def send_second():
+        local[4].wait()
+        target_out[...] = jnp.round((measured[0] - MIDDLE) * SCALE).astype(jnp.int32).astype(jnp.int16)
+        pl.semaphore_wait(turn_sem, 1)
+        code_copy.start()
+        target_copy.start()
+        code_copy.wait_send()
+
+    @pl.when(cut == 0)
+    def rest():
+        local[4].wait()
+
     off_copy.wait()
-    next_at = off_in[0:1, 0:1]
-    pick = one_hot((cols, width), 0, next_at)
-    picked = dot(high, pick) + dot(low, pick)
-    level = jnp.maximum(jnp.max(jnp.abs(picked), axis=0, keepdims=True), 1e-30) * (1.0 / 32767.0)
-    level_out[...] = jnp.broadcast_to(level, level_out.shape)
-    level_copy = remote(level_out, level_in, 1, (cut, before))
-    level_copy.start()
-    code_out[...] = jnp.round(picked / level).astype(jnp.int32).astype(jnp.int16)
-    code_copy = remote(code_out, code_in, 2, (cut, before))
-    code_copy.start()
-
-    pick = one_hot((cols, width), 0, col_at)
-    mine = beside(dot(high, pick) + dot(low, pick))
-    mine = moved_left(one_hot((width, rows), 1, row_at), mine)
-    row_pick = one_hot((width, rows), 1, row_at, rows)
+    their_row = off_in[0:1, 0:1]
+    their_col = off_in[1:2, 0:1]
+    flag = jnp.where(off_in[2:3, 0:1] > 0, 1.0, 0.0)
+    pick = one_hot((cols, width), 0, their_col)
+    mine = beside(moved_right(jnp.concatenate([trans[0], trans[1]], axis=0), pick))
+    mine = moved_left(one_hot((width, rows), 1, their_row, rows), mine)
+    row_pick = one_hot((width, rows), 1, their_row)
+    local[3].wait()
+    local[5].wait()
     level_copy.wait()
-    code_copy.wait()
+    code_copy.wait_recv()
     theirs = code_in[...].astype(jnp.int32).astype(F32) * level_in[0:1]
     patch = mine + moved_left(row_pick, beside(theirs))
     obj_r, obj_i = patch[:, :width], patch[:, width:]
@@ -221,7 +247,9 @@
         value = from_right(jnp.concatenate([chi_r, chi_i], axis=1), mats, 0)
         value = from_left(above(value), mats, 2)
         out_r, out_i = value[:width], value[width:]
-        weight = (out_r * out_r + out_i * out_i - measured[0]) * flag
+        target_copy.wait()
+        target = target_in[...].astype(jnp.int32).astype(F32) * (1.0 / SCALE) + MIDDLE
+        weight = (out_r * out_r + out_i * out_i - target) * flag
         value = jnp.concatenate([weight * out_r, weight * out_i], axis=0)
         value = from_left(value, mats, 0)
         value = from_right(beside(value), mats, 2)
@@ -234,13 +262,13 @@
 
     total = grads[...]
     high, low = halves(total)
-    spill_out[...] = dot(one_hot((rows, width), 0, row_at, rows), high).astype(BF16)
-    spill = remote(spill_out, spill_in, 5, (cut, after))
+    spill_out[...] = dot(one_hot((rows, width), 0, their_row), high).astype(BF16)
+    spill = remote(spill_out, spill_in, 5, (cut, before))
     spill.start()
-    row_put = one_hot((rows, width), 0, row_at)
+    row_put = one_hot((rows, width), 0, their_row, rows)
     kept = above(dot(row_put, high) + dot(row_put, low))
-    kept = moved_right(kept, one_hot((width, cols), 1, col_at))
-    put = one_hot((width, cols), 1, off_in[0:1, 0:1])
+    kept = moved_right(kept, one_hot((width, cols), 1, their_col))
+    put = one_hot((width, cols), 1, col_at)
     spill.wait()
     for part in range(2):
         arrived = dot(spill_in[:, part * width : (part + 1) * width], put)
@@ -277,12 +305,15 @@
             pltpu.VMEM((width, 2 * width), F32),
             pltpu.VMEM((rows, 2 * width), BF16),
             pltpu.VMEM((rows, 2 * width), BF16),
+            pltpu.VMEM((width, width), jnp.int16),
+            pltpu.VMEM((width, width), jnp.int16),
+            pltpu.SemaphoreType.REGULAR,
             pltpu.SemaphoreType.DMA((6,)),
-            pltpu.SemaphoreType.DMA((6,)),
-            pltpu.SemaphoreType.DMA((6,)),
+            pltpu.SemaphoreType.DMA((7,)),
+            pltpu.SemaphoreType.DMA((7,)),
         ],
         compiler_params=pltpu.CompilerParams(
-            collective_id=0, has_side_effects=True, vmem_limit_bytes=48 * 1024 * 1024
+            collective_id=0, has_side_effects=True, vmem_limit_bytes=60 * 1024 * 1024
         ),
     )(trans, illumination, measured, offsets, live_count[:, None], jnp.asarray(tables))
     return total[:, None]

time: 41.9 us -> 32.7 us (0.78)
  Pallas kernels: 36.1 us -> 29.6 us
  local copies, waits for them, and re-layouts: 4.84 us -> 2.26 us
    pallas_call x1, Pallas kernels: 36.1 us -> 29.6 us  [on_device(): pl.pallas_call(functools.partial(kernel, tiles), out_shape=jax.ShapeDtype...]
    unnamed x9 -> x1, local copies, waits for them, and re-layouts: 4.84 us -> 2.26 us
where the time goes in v2:
time: 32.7 us; the launch traced here: 32.5 us
  Pallas kernels  29.6 us (91%)
  local copies, waits for them, and re-layouts  2.26 us (7%)
  between operations  0.66 us (2%)
    pallas_call x1, Pallas kernels, on_device(): pl.pallas_call(functools.partial(kernel, tiles), out_shape=jax.ShapeDtype...  29.6 us
    unnamed x1, local copies, waits for them, and re-layouts  2.26 us

profile of v2, /device:TPU:0, one launch (start us, length us, event | category | flops | bytes accessed | tf_op | source)
XLA Modules:
  0.0 32.5 jit_solution(9026784063764099504)
XLA Ops:
  0.7 29.6 %shard_map.64 = f32[2,256,512]{2,1,0:T(8,128)} custom-call(f32[2,256,512]{2,1,0:T(8,128)} %bitcast.7, f32[2,256,256]{2,1,0:T(8,128)} %illum_hbm.1, f32[1,256,256]{2,1,0:T(8,128)} %measured_hbm.1, s32[1,2]{1,0:T(1,128)} %offs_hbm.1, s32[1,1]{1,0:T(1,128)} %bitcast.5.live_hbm, bf16[2,4,512,512]{3,2,1,0:T(8,128)(2,1)} %constant.2.clone.tables), custom_call_target="tpu_custom_call" | custom-call | tf_op jit(solution)/shard_map/pallas_call | solution.py:283
  30.2 2.3 %copy.10 = f32[2,1,256,512]{3,2,1,0:T(8,128)} copy(f32[2,1,256,512]{3,2,1,0:T(8,128)} %bitcast.6) | data formatting | bytes 2097152

commit v3 on v2

--- a/solution.py
+++ b/solution.py
@@ -15,6 +15,7 @@
 BF16 = jnp.bfloat16
 MIDDLE = 2.6
 SCALE = 13650.0
+PARTS = 2
 
 
 def split_pair(value):
@@ -50,7 +51,9 @@
 
 def from_right(value, mats, at):
     high, low = halves(value)
-    return dot(high, mats[at]) + (dot(low, mats[at]) + dot(high, mats[at + 1]))
+    count = value.shape[0]
+    both = dot(jnp.concatenate([high, low], axis=0), mats[at])
+    return both[:count] + (both[count:] + dot(high, mats[at + 1]))
 
 
 def from_left(value, mats, at):
@@ -148,7 +151,8 @@
         (tables.at[cut], mats),
     ):
         copy = pltpu.make_async_copy(source, target, local_sem.at[len(local)])
-        copy.start()
+        if len(local) < 3:
+            copy.start()
         local.append(copy)
     local[0].wait()
     local[1].wait()
@@ -156,13 +160,7 @@
     col_at = offs[0:1, 1:2]
     line = lax.broadcasted_iota(jnp.int32, off_out.shape, 0)
     off_out[...] = jnp.where(line == 0, row_at, jnp.where(line == 1, col_at, live[0:1, 0:1]))
-    local[2].wait()
     pick = one_hot((cols, width), 0, col_at)
-    picked = moved_right(jnp.concatenate([trans[0], trans[1]], axis=0), pick)
-    level = jnp.maximum(jnp.max(jnp.abs(picked), axis=0, keepdims=True), 1e-30) * (1.0 / 32767.0)
-    level_out[...] = jnp.broadcast_to(level, level_out.shape)
-    code_out[...] = jnp.round(picked / level).astype(jnp.int32).astype(jnp.int16)
-    pl.semaphore_wait(barrier, 2)
 
     def remote(src, dst, at, target):
         return pltpu.make_async_remote_copy(
@@ -174,31 +172,42 @@
             device_id_type=MESH,
         )
 
+    def per_part(src, dst, first, target):
+        return [remote(src.at[c], dst.at[c], first + c, target) for c in range(PARTS)]
+
     off_copy = remote(off_out, off_in, 0, (cut, after))
-    off_copy.start()
-    level_copy = remote(level_out, level_in, 1, (cut, after))
-    level_copy.start()
-    code_copy = remote(code_out, code_in, 2, (cut, after))
-    target_copy = remote(target_out, target_in, 6, (1, after))
-
-    @pl.when(cut == 0)
-    def send_first():
-        code_copy.start()
-        code_copy.wait_send()
-        pl.semaphore_signal(turn_sem, inc=1, device_id=(other, tile), device_id_type=MESH)
+    target_copy = remote(target_out, target_in, 1, (1, after))
+    level_copies = per_part(level_out, level_in, 2, (cut, after))
+    code_copies = per_part(code_out, code_in, 2 + PARTS, (cut, after))
+    wave_copies = per_part(wave_out, wave, 2 + 2 * PARTS, (1, tile))
+    back_copies = per_part(back_out, back, 2 + 3 * PARTS, (0, tile))
+    spill_copies = per_part(spill_out, spill_in, 2 + 4 * PARTS, (cut, before))
+
+    local[2].wait()
+    for copy in local[3:]:
+        copy.start()
+    strip = rows // PARTS
+    for c in range(PARTS):
+        part = slice(c * strip, (c + 1) * strip)
+        picked = moved_right(jnp.concatenate([trans[0, part], trans[1, part]], axis=0), pick)
+        peak = jnp.maximum(jnp.max(jnp.abs(picked), axis=0, keepdims=True), 1e-30)
+        level_out[c] = jnp.broadcast_to(peak * (1.0 / 32766.0), level_out.shape[1:])
+        code = jnp.round(picked * (32766.0 / peak))
+        code_out[c] = code.astype(jnp.int32).astype(jnp.int16)
+        if c == 0:
+            pl.semaphore_wait(barrier, 2)
+            off_copy.start()
+        level_copies[c].start()
+
+        @pl.when(cut == 0)
+        def send_first():
+            code_copies[c].start()
 
     @pl.when(cut == 1)
-    def send_second():
+    def code_target():
         local[4].wait()
-        target_out[...] = jnp.round((measured[0] - MIDDLE) * SCALE).astype(jnp.int32).astype(jnp.int16)
-        pl.semaphore_wait(turn_sem, 1)
-        code_copy.start()
-        target_copy.start()
-        code_copy.wait_send()
-
-    @pl.when(cut == 0)
-    def rest():
-        local[4].wait()
+        moved = jnp.round((measured[0] - MIDDLE) * SCALE)
+        target_out[...] = moved.astype(jnp.int32).astype(jnp.int16)
 
     off_copy.wait()
     their_row = off_in[0:1, 0:1]
@@ -206,73 +215,103 @@
     flag = jnp.where(off_in[2:3, 0:1] > 0, 1.0, 0.0)
     pick = one_hot((cols, width), 0, their_col)
     mine = beside(moved_right(jnp.concatenate([trans[0], trans[1]], axis=0), pick))
-    mine = moved_left(one_hot((width, rows), 1, their_row, rows), mine)
+    patch = moved_left(one_hot((width, rows), 1, their_row, rows), mine)
     row_pick = one_hot((width, rows), 1, their_row)
     local[3].wait()
     local[5].wait()
-    level_copy.wait()
-    code_copy.wait_recv()
-    theirs = code_in[...].astype(jnp.int32).astype(F32) * level_in[0:1]
-    patch = mine + moved_left(row_pick, beside(theirs))
+
+    @pl.when(cut == 0)
+    def pass_turn():
+        for copy in code_copies:
+            copy.wait_send()
+        pl.semaphore_signal(turn_sem, inc=1, device_id=(other, tile), device_id_type=MESH)
+        local[4].wait()
+
+    @pl.when(cut == 1)
+    def take_turn():
+        pl.semaphore_wait(turn_sem, 1)
+        for copy in code_copies:
+            copy.start()
+        target_copy.start()
+
+    for c in range(PARTS):
+        level_copies[c].wait()
+        code_copies[c].wait_recv()
+        theirs = code_in[c].astype(jnp.int32).astype(F32) * level_in[c, 0:1]
+        patch = patch + moved_left(row_pick[:, c * strip : (c + 1) * strip], beside(theirs))
     obj_r, obj_i = patch[:, :width], patch[:, width:]
-
-    wave_copy = remote(wave_out, wave, 3, (1, tile))
-    back_copy = remote(back_out, back, 4, (0, tile))
-
-    def keep_grads(psi_r, psi_i, h_r, h_i):
-        grad_r, grad_i = conj_times(psi_r, psi_i, h_r, h_i)
-        grads[:, :width] = grad_r
-        grads[:, width:] = grad_i
+    step = width // PARTS
+    parts = [slice(c * step, (c + 1) * step) for c in range(PARTS)]
+
+    def keep_grads(c, psi_r, psi_i, h_r, h_i):
+        grad = jnp.concatenate(conj_times(psi_r, psi_i, h_r, h_i), axis=1)
+        grads[parts[c]] = grad
+        spill_out[c] = grad.astype(BF16)
+        spill_copies[c].start()
 
     @pl.when(cut == 0)
     def first():
         chi_r, chi_i = times(illum[0], illum[1], obj_r, obj_i)
-        value = from_left(jnp.concatenate([chi_r, chi_i], axis=0), mats, 2)
-        value = from_right(beside(value), mats, 0)
-        wave_out[...] = value.astype(BF16)
-        wave_copy.start()
-        wave_copy.wait_send()
-        back_copy.wait_recv()
-        grad = back[...]
-        value = dot(grad, mats[2]) + dot(grad, mats[3])
-        value = from_left(above(value), mats, 0)
-        keep_grads(illum[0], illum[1], value[:width], value[width:])
+        value = beside(from_left(jnp.concatenate([chi_r, chi_i], axis=0), mats, 2))
+        for c in range(PARTS):
+            wave_out[c] = from_right(value[parts[c]], mats, 0).astype(BF16)
+            wave_copies[c].start()
+        values = []
+        for c in range(PARTS):
+            back_copies[c].wait_recv()
+            grad = back[c]
+            values.append(dot(grad, mats[2]) + dot(grad, mats[3]))
+        high, low = halves(above(jnp.concatenate(values, axis=0)))
+        for c in range(PARTS):
+            lead = [
+                jnp.concatenate([mats[at, parts[c]], mats[at, pl.ds(width + c * step, step)]], axis=0)
+                for at in range(2)
+            ]
+            value = dot(lead[0], high) + (dot(lead[0], low) + dot(lead[1], high))
+            keep_grads(c, illum[0, parts[c]], illum[1, parts[c]], value[:step], value[step:])
+        for copy in wave_copies:
+            copy.wait_send()
 
     @pl.when(cut == 1)
     def second():
-        wave_copy.wait_recv()
-        psi = wave[...].astype(F32)
-        psi_r, psi_i = psi[:, :width], psi[:, width:]
-        chi_r, chi_i = times(psi_r, psi_i, obj_r, obj_i)
-        value = from_right(jnp.concatenate([chi_r, chi_i], axis=1), mats, 0)
-        value = from_left(above(value), mats, 2)
+        values, waves = [], []
+        for c in range(PARTS):
+            wave_copies[c].wait_recv()
+            psi = wave[c].astype(F32)
+            psi_r, psi_i = psi[:, :width], psi[:, width:]
+            chi = times(psi_r, psi_i, obj_r[parts[c]], obj_i[parts[c]])
+            values.append(from_right(jnp.concatenate(chi, axis=1), mats, 0))
+            waves.append((psi_r, psi_i))
+        value = from_left(above(jnp.concatenate(values, axis=0)), mats, 2)
         out_r, out_i = value[:width], value[width:]
         target_copy.wait()
         target = target_in[...].astype(jnp.int32).astype(F32) * (1.0 / SCALE) + MIDDLE
         weight = (out_r * out_r + out_i * out_i - target) * flag
         value = jnp.concatenate([weight * out_r, weight * out_i], axis=0)
-        value = from_left(value, mats, 0)
-        value = from_right(beside(value), mats, 2)
-        h_r, h_i = value[:, :width], value[:, width:]
-        g_r, g_i = conj_times(obj_r, obj_i, h_r, h_i)
-        back_out[...] = jnp.concatenate([g_r, g_i], axis=1).astype(BF16)
-        back_copy.start()
-        keep_grads(psi_r, psi_i, h_r, h_i)
-        back_copy.wait_send()
-
-    total = grads[...]
-    high, low = halves(total)
-    spill_out[...] = dot(one_hot((rows, width), 0, their_row), high).astype(BF16)
-    spill = remote(spill_out, spill_in, 5, (cut, before))
-    spill.start()
+        value = beside(from_left(value, mats, 0))
+        for c in range(PARTS):
+            back_wave = from_right(value[parts[c]], mats, 2)
+            h_r, h_i = back_wave[:, :width], back_wave[:, width:]
+            g = conj_times(obj_r[parts[c]], obj_i[parts[c]], h_r, h_i)
+            back_out[c] = jnp.concatenate(g, axis=1).astype(BF16)
+            back_copies[c].start()
+            keep_grads(c, *waves[c], h_r, h_i)
+        for copy in back_copies + code_copies:
+            copy.wait_send()
+
+    high, low = halves(grads[...])
     row_put = one_hot((rows, width), 0, their_row, rows)
     kept = above(dot(row_put, high) + dot(row_put, low))
     kept = moved_right(kept, one_hot((width, cols), 1, their_col))
     put = one_hot((width, cols), 1, col_at)
-    spill.wait()
+    row_take = one_hot((rows, width), 0, row_at)
+    arrived = jnp.zeros((rows, 2 * width), F32)
+    for c in range(PARTS):
+        spill_copies[c].wait()
+        arrived = arrived + dot(row_take[:, parts[c]], spill_in[c])
+    arrived = dot(above(arrived).astype(BF16), put) + kept
     for part in range(2):
-        arrived = dot(spill_in[:, part * width : (part + 1) * width], put)
-        out[part] = kept[part * rows : (part + 1) * rows] + arrived
+        out[part] = arrived[part * rows : (part + 1) * rows]
 
 
 def on_device(tiles, tables, transmission, illumination, measured, offsets, live_count):
@@ -282,7 +321,7 @@
     hbm = pl.BlockSpec(memory_space=pltpu.HBM)
     total = pl.pallas_call(
         functools.partial(kernel, tiles),
-        out_shape=jax.ShapeDtypeStruct(trans.shape, F32),
+        out_shape=pltpu.VMEM(trans.shape, F32),
         in_specs=[hbm] * 6,
         out_specs=pl.BlockSpec(memory_space=pltpu.VMEM),
         scratch_shapes=[
@@ -294,23 +333,23 @@
             pltpu.VMEM((4, 2 * width, 2 * width), BF16),
             pltpu.VMEM((8, 128), jnp.int32),
             pltpu.VMEM((8, 128), jnp.int32),
-            pltpu.VMEM((2 * rows, width), jnp.int16),
-            pltpu.VMEM((2 * rows, width), jnp.int16),
-            pltpu.VMEM((8, width), F32),
-            pltpu.VMEM((8, width), F32),
-            pltpu.VMEM((width, 2 * width), BF16),
-            pltpu.VMEM((width, 2 * width), BF16),
-            pltpu.VMEM((width, 2 * width), BF16),
-            pltpu.VMEM((width, 2 * width), BF16),
+            pltpu.VMEM((PARTS, 2 * rows // PARTS, width), jnp.int16),
+            pltpu.VMEM((PARTS, 2 * rows // PARTS, width), jnp.int16),
+            pltpu.VMEM((PARTS, 8, width), F32),
+            pltpu.VMEM((PARTS, 8, width), F32),
+            pltpu.VMEM((PARTS, width // PARTS, 2 * width), BF16),
+            pltpu.VMEM((PARTS, width // PARTS, 2 * width), BF16),
+            pltpu.VMEM((PARTS, width // PARTS, 2 * width), BF16),
+            pltpu.VMEM((PARTS, width // PARTS, 2 * width), BF16),
             pltpu.VMEM((width, 2 * width), F32),
-            pltpu.VMEM((rows, 2 * width), BF16),
-            pltpu.VMEM((rows, 2 * width), BF16),
+            pltpu.VMEM((PARTS, width // PARTS, 2 * width), BF16),
+            pltpu.VMEM((PARTS, width // PARTS, 2 * width), BF16),
             pltpu.VMEM((width, width), jnp.int16),
             pltpu.VMEM((width, width), jnp.int16),
             pltpu.SemaphoreType.REGULAR,
             pltpu.SemaphoreType.DMA((6,)),
-            pltpu.SemaphoreType.DMA((7,)),
-            pltpu.SemaphoreType.DMA((7,)),
+            pltpu.SemaphoreType.DMA((2 + 5 * PARTS,)),
+            pltpu.SemaphoreType.DMA((2 + 5 * PARTS,)),
         ],
         compiler_params=pltpu.CompilerParams(
             collective_id=0, has_side_effects=True, vmem_limit_bytes=60 * 1024 * 1024

time: 32.7 us -> 29.6 us (0.905)
  Pallas kernels: 29.6 us -> 27.8 us
  local copies, waits for them, and re-layouts: 2.26 us -> 0.97 us
    pallas_call x1, Pallas kernels: 29.6 us -> 27.8 us  [on_device(): pl.pallas_call(functools.partial(kernel, tiles), out_shape=pltpu.VMEM(tra...]
    unnamed x1, local copies, waits for them, and re-layouts: 2.26 us -> 0.97 us
where the time goes in v3:
time: 29.6 us; the launch traced here: 29.5 us
  Pallas kernels  27.8 us (94%)
  local copies, waits for them, and re-layouts  0.97 us (3%)
  between operations  0.66 us (2%)
    pallas_call x1, Pallas kernels, on_device(): pl.pallas_call(functools.partial(kernel, tiles), out_shape=pltpu.VMEM(tra...  27.8 us
    unnamed x1, local copies, waits for them, and re-layouts  0.97 us

profile of v3, /device:TPU:0, one launch (start us, length us, event | category | flops | bytes accessed | tf_op | source)
XLA Modules:
  0.0 29.5 jit_solution(4506064789526236346)
XLA Ops:
  0.7 27.8 %shard_map.64 = f32[2,256,512]{2,1,0:T(8,128)S(1)} custom-call(f32[2,256,512]{2,1,0:T(8,128)} %bitcast.7, f32[2,256,256]{2,1,0:T(8,128)} %illum_hbm.1, f32[1,256,256]{2,1,0:T(8,128)} %measured_hbm.1, s32[1,2]{1,0:T(1,128)} %offs_hbm.1, s32[1,1]{1,0:T(1,128)} %bitcast.5.live_hbm, bf16[2,4,512,512]{3,2,1,0:T(8,128)(2,1)} %constant.2.clone.tables), custom_call_target="tpu_custom_call" | custom-call | tf_op jit(solution)/shard_map/pallas_call | solution.py:322
  28.5 1.0 %copy.9 = f32[2,1,256,512]{3,2,1,0:T(8,128)} copy(f32[2,1,256,512]{3,2,1,0:T(8,128)S(1)} %bitcast.6) | data formatting | bytes 2097152
